TPU v7x, 32 devices: a whole 2x2x4 slice. The times are simulated.
32 devices in a mesh: group: 2 (over y), pre: 4 (over z), head: 2 (over x), sub: 2 (over core).
Axes of the slice: x: 2, y: 2, z: 4, core: 2. Of those that a mesh axis runs over, the one named last changes fastest.
Arguments:
- prefix_query: bfloat16 [8, 256, 2048], P(('group', 'pre'), None, ('head', 'sub')), parts along dimension 0, may hold values from -0.5390625 to 0.5390625
- prefix_key: bfloat16 [8, 256, 2048], P(('group', 'pre'), None, ('head', 'sub')), parts along dimension 0, may hold values from -0.5390625 to 0.5390625
- prefix_value: bfloat16 [8, 256, 2048], P(('group', 'pre'), None, ('head', 'sub')), parts along dimension 0, may hold values from -6 to 6
- prefix_decay: float32 [8, 16, 256], P(('group', 'pre'), ('head', 'sub')), parts along dimension 0, may hold values from -3 to 0
- prefix_beta: float32 [8, 16, 256], P(('group', 'pre'), ('head', 'sub')), parts along dimension 0, may hold values from 0.1 to 0.9
- prefix_cotangent: bfloat16 [8, 256, 2048], P(('group', 'pre'), None, ('head', 'sub')), parts along dimension 0, may hold values from -6 to 6
- branch_query: bfloat16 [32, 128, 2048], P(('group', 'pre'), None, ('head', 'sub')), parts along dimension 0, may hold values from -0.5390625 to 0.5390625
- branch_key: bfloat16 [32, 128, 2048], P(('group', 'pre'), None, ('head', 'sub')), parts along dimension 0, may hold values from -0.5390625 to 0.5390625
- branch_value: bfloat16 [32, 128, 2048], P(('group', 'pre'), None, ('head', 'sub')), parts along dimension 0, may hold values from -6 to 6
- branch_decay: float32 [32, 16, 128], P(('group', 'pre'), ('head', 'sub')), parts along dimension 0, may hold values from -3 to 0
- branch_beta: float32 [32, 16, 128], P(('group', 'pre'), ('head', 'sub')), parts along dimension 0, may hold values from 0.1 to 0.9
- branch_cotangent: bfloat16 [32, 128, 2048], P(('group', 'pre'), None, ('head', 'sub')), parts along dimension 0, may hold values from -6 to 6
- fanout: int32 [8], P('group'), parts along dimension 0, may hold values from 2 to 10, as said below
- placement: int32 [32], P(('group', 'pre')), parts along dimension 0, may hold values from 0 to 15, each once
Outputs:
- branch_out: bfloat16 [32, 128, 2048], P(('group', 'pre'), None, ('head', 'sub')), parts along dimension 0
- trunk_query: bfloat16 [8, 256, 2048], P(('group', 'pre'), None, ('head', 'sub')), parts along dimension 0
- trunk_key: bfloat16 [8, 256, 2048], P(('group', 'pre'), None, ('head', 'sub')), parts along dimension 0
- trunk_value: bfloat16 [8, 256, 2048], P(('group', 'pre'), None, ('head', 'sub')), parts along dimension 0
- trunk_decay: float32 [8, 16, 256], P(('group', 'pre'), ('head', 'sub')), parts along dimension 0
- trunk_beta: float32 [8, 16, 256], P(('group', 'pre'), ('head', 'sub')), parts along dimension 0
- limb_query: bfloat16 [32, 128, 2048], P(('group', 'pre'), None, ('head', 'sub')), parts along dimension 0
- limb_key: bfloat16 [32, 128, 2048], P(('group', 'pre'), None, ('head', 'sub')), parts along dimension 0
- limb_value: bfloat16 [32, 128, 2048], P(('group', 'pre'), None, ('head', 'sub')), parts along dimension 0
- limb_decay: float32 [32, 16, 128], P(('group', 'pre'), ('head', 'sub')), parts along dimension 0
- limb_beta: float32 [32, 16, 128], P(('group', 'pre'), ('head', 'sub')), parts along dimension 0
There are 2 independent parts, one for each index of `group`. A program takes and returns all parts, laid end to end along the dimension named above; each array names one. Nothing has to cross between parts.
Inputs may be any that keep to these rules, and one draw needn't show every extreme that they name: `fanout`: every prefix has at least 2 branches, the counts sum to 16, and some prefix has exactly 10. `placement`: the branches of prefix p have the ranks from bounds_(p-1) (0 for the first) up to bounds_p - 1.
All inputs are finite; a program needn't handle non-finite values.
Results may differ from a plain program's by a relative error of at most 0.015.
Values sent between devices are 32-bit elements; how exact they have to be, the bound alone decides.
A program may use at most 192 MiB of HBM per device.

v0:
```python
import functools

import jax
import jax.numpy as jnp
from jax import lax
from jax.experimental import pallas as pl
from jax.experimental.pallas import tpu as pltpu
from jax.sharding import PartitionSpec as P

SPAN = 128
F32 = jnp.float32
BF16 = jnp.bfloat16
HIGH = lax.Precision.HIGHEST
VMEM_BYTES = 40 * 1024 * 1024


def mm(a, b, ca, cb):
    return lax.dot_general(
        a.astype(BF16), b.astype(BF16), (((ca,), (cb,)), ((), ())), preferred_element_type=F32
    )


def nn(a, b):
    return mm(a, b, 1, 0)


def nt(a, b):
    return mm(a, b, 1, 1)


def tn(a, b):
    return mm(a, b, 0, 0)


def exact(a, b, ca, cb):
    return lax.dot_general(
        a, b, (((ca,), (cb,)), ((), ())), precision=HIGH, preferred_element_type=F32
    )


def grid_pair():
    row = lax.broadcasted_iota(jnp.int32, (SPAN, SPAN), 0)
    col = lax.broadcasted_iota(jnp.int32, (SPAN, SPAN), 1)
    return row, col


def rows_total(x):
    return jnp.sum(x, axis=-1, keepdims=True)


def unit(x):
    wide = x.astype(F32)
    scale = lax.rsqrt(rows_total(wide * wide) + 1e-06)
    full = wide * scale
    return scale, full, full.astype(BF16)


def unit_back(scale, full, grad):
    grad = grad.astype(BF16).astype(F32)
    return (scale * (grad - full * rows_total(full * grad))).astype(BF16)


def token_vectors(decay, beta):
    row, col = grid_pair()
    lower = (row >= col).astype(F32)
    sums_col = exact(lower, decay, 1, 1)
    sums_row = exact(decay, lower, 1, 1)
    beta_col = exact((row == col).astype(F32), beta, 1, 1)
    return sums_col, sums_row, beta_col


def ratio_of(g_col, g_row):
    row, col = grid_pair()
    return jnp.where(row >= col, jnp.exp(jnp.minimum(g_col - g_row, 0.0)), 0.0)


def strict_part(x):
    row, col = grid_pair()
    return jnp.where(row > col, x, 0.0)


def inverses(mixings):
    row, col = grid_pair()
    apart = row ^ col
    low = [a.astype(BF16) for a in mixings]
    zero = jnp.zeros((SPAN, SPAN), BF16)
    one = (row == col).astype(BF16)
    inv = [one - jnp.where(apart == 1, a, zero) for a in low]
    size = 2
    while size < SPAN:
        band = (apart >= size) & (apart < 2 * size)
        left = [nn(t, jnp.where(band, a, zero)) for t, a in zip(inv, low)]
        inv = [t - nn(y, t).astype(BF16) for t, y in zip(inv, left)]
        size *= 2
    return inv


def prefix_forward_kernel(heads, blocks, k_ref, v_ref, g_ref, b_ref, state_ref, mid_ref, u_ref, t_ref):
    vecs = [
        token_vectors(g_ref[0, :, pl.ds(n * SPAN, SPAN)], b_ref[0, :, pl.ds(n * SPAN, SPAN)])
        for n in range(blocks)
    ]
    units = [(h, n) for n in range(blocks) for h in range(heads)]
    keys, mixings = {}, []
    for h, n in units:
        sums_col, sums_row, beta_col = vecs[n]
        _, _, key = unit(k_ref[0, pl.ds(n * SPAN, SPAN), pl.ds(h * 128, 128)])
        keys[h, n] = key
        ratio = ratio_of(sums_col[:, h : h + 1], sums_row[h : h + 1, :])
        mixings.append(strict_part(beta_col[:, h : h + 1] * ratio * nt(key, key)))
    inv = dict(zip(units, inverses(mixings)))
    for h, n in units:
        t_ref[n, h] = inv[h, n]
    state = {}
    for n in range(blocks):
        sums_col, sums_row, beta_col = vecs[n]
        for h in range(heads):
            g_col, beta = sums_col[:, h : h + 1], beta_col[:, h : h + 1]
            last = g_col[SPAN - 1 : SPAN, :]
            aim = v_ref[0, pl.ds(n * SPAN, SPAN), pl.ds(h * 128, 128)].astype(F32)
            if n > 0:
                mid_ref[n - 1, h] = state[h]
                aim = aim - jnp.exp(g_col) * nn(keys[h, n], state[h])
            update = nn(inv[h, n], beta * aim)
            u_ref[0, pl.ds(n * SPAN, SPAN), pl.ds(h * 128, 128)] = update.astype(BF16)
            new = tn(keys[h, n].astype(F32) * jnp.exp(last - g_col), update)
            state[h] = new if n == 0 else jnp.exp(last) * state[h] + new
    for h in range(heads):
        state_ref[0, h] = state[h]


def branch_pull_kernel(
    heads, parent_ref, q_ref, k_ref, d_ref, g_ref, b_ref, sums_ref, t_ref, x_ref, dv_ref
):
    j = pl.program_id(0)

    @pl.when(j == 0)
    def _():
        sums_ref[...] = jnp.zeros_like(sums_ref)

    sums_col, sums_row, beta_col = token_vectors(g_ref[0], b_ref[0])
    both, mixings, scores = [], [], []
    for h in range(heads):
        lanes = pl.ds(h * 128, 128)
        _, _, query = unit(q_ref[0, :, lanes])
        _, _, key = unit(k_ref[0, :, lanes])
        pair = jnp.concatenate([query, key], axis=0)
        gram = nt(pair, key)
        ratio = ratio_of(sums_col[:, h : h + 1], sums_row[h : h + 1, :])
        scores.append((gram[:SPAN] * ratio).astype(BF16))
        mixings.append(strict_part(beta_col[:, h : h + 1] * ratio * gram[SPAN:]))
        both.append(pair)
    pulled = [tn(s, d_ref[0, :, pl.ds(h * 128, 128)]) for h, s in enumerate(scores)]
    inv = inverses(mixings)
    target = [tn(t, u) for t, u in zip(inv, pulled)]
    for h in range(heads):
        lanes = pl.ds(h * 128, 128)
        beta = beta_col[:, h : h + 1]
        growth = jnp.exp(sums_col[:, h : h + 1])
        slope = beta * target[h]
        t_ref[0, h] = inv[h]
        x_ref[0, :, lanes] = target[h].astype(BF16)
        dv_ref[0, :, lanes] = slope.astype(BF16)
        cot = d_ref[0, :, lanes].astype(F32)
        right = jnp.concatenate([(growth * cot).astype(BF16), (-growth * slope).astype(BF16)], axis=0)
        sums_ref[parent_ref[j], h] += tn(both[h], right)


def finish(query, key, state, inv_x, beta, g_col, g_row, values, update, cot, dx, next_grad):
    pair = jnp.concatenate([query, key], axis=0)
    gram = nt(pair, key)
    score_gram, key_gram = gram[:SPAN], gram[SPAN:]
    ratio = ratio_of(g_col, g_row)
    growth = jnp.exp(g_col)
    out = None
    aim = values
    if state is not None:
        seen = nn(pair, state)
        aim = values - growth * seen[SPAN:]
    if update is None:
        update = nn(inv_x, beta * aim)
        out = nn(score_gram * ratio, update) + growth * seen[:SPAN]
    grads = jnp.concatenate([cot, dx.astype(BF16)], axis=0)
    outer = nt(grads, update)
    d_score = outer[:SPAN] * ratio
    d_mix = strict_part(outer[SPAN:] * (-beta * ratio))
    stack = jnp.concatenate([d_score.astype(BF16), d_mix.astype(BF16)], axis=0)
    down = nn(stack, key)
    d_query = down[:SPAN]
    d_key = down[SPAN:] + tn(stack, pair)
    mix_part = d_mix * key_gram
    d_ratio = d_score * score_gram + mix_part
    wide_dx = dx.astype(F32)
    d_beta = rows_total(wide_dx * aim + mix_part / beta)
    column = d_ratio
    constant = None
    if state is not None:
        back = nt(grads, state)
        d_query = d_query + growth * back[:SPAN]
        slope = beta * growth
        d_key = d_key - slope * back[SPAN:]
        column = column + growth * (cot.astype(F32) * seen[:SPAN]) - slope * (wide_dx * seen[SPAN:])
    if next_grad is not None:
        last = g_col[SPAN - 1 : SPAN, :]
        trail = jnp.exp(last - g_col) * nt(update, next_grad)
        d_key = d_key + trail
        trailing = trail * key.astype(F32)
        column = column - trailing
        constant = jnp.sum(rows_total(trailing), axis=0, keepdims=True)
        if state is not None:
            product = jnp.sum(rows_total(state * next_grad), axis=0, keepdims=True)
            constant = constant + jnp.exp(last) * product
    return d_query, d_key, d_beta, rows_total(column), jnp.sum(d_ratio, axis=0, keepdims=True), constant, out


def token_rows(columns, rows, betas):
    row, col = grid_pair()
    lower = (row >= col).astype(F32)
    d_decay = exact(jnp.concatenate(columns, axis=1), lower, 0, 0) - exact(
        jnp.concatenate(rows, axis=0), lower, 1, 0
    )
    d_beta = exact(jnp.concatenate(betas, axis=1), (row == col).astype(F32), 0, 0)
    return d_decay, d_beta


def branch_finish_kernel(
    heads, parent_ref, q_ref, k_ref, v_ref, d_ref, g_ref, b_ref, t_ref, x_ref, s_ref,
    o_ref, dq_ref, dk_ref, dg_ref, db_ref,
):
    sums_col, sums_row, beta_col = token_vectors(g_ref[0], b_ref[0])
    columns, rows, betas = [], [], []
    for h in range(heads):
        lanes = pl.ds(h * 128, 128)
        q_scale, q_full, query = unit(q_ref[0, :, lanes])
        k_scale, k_full, key = unit(k_ref[0, :, lanes])
        d_query, d_key, d_beta, column, row, _, out = finish(
            query, key, s_ref[0, h], t_ref[0, h], beta_col[:, h : h + 1],
            sums_col[:, h : h + 1], sums_row[h : h + 1, :], v_ref[0, :, lanes].astype(F32),
            None, d_ref[0, :, lanes], x_ref[0, :, lanes], None,
        )
        o_ref[0, :, lanes] = out.astype(BF16)
        dq_ref[0, :, lanes] = unit_back(q_scale, q_full, d_query)
        dk_ref[0, :, lanes] = unit_back(k_scale, k_full, d_key)
        columns.append(column)
        rows.append(row)
        betas.append(d_beta)
    d_decay, d_beta = token_rows(columns, rows, betas)
    dg_ref[0] = d_decay
    db_ref[0] = d_beta


def prefix_finish_kernel(
    heads, blocks, q_ref, k_ref, v_ref, d_ref, g_ref, b_ref, t_ref, u_ref, mid_ref, sg_ref,
    dq_ref, dk_ref, dv_ref, dg_ref, db_ref,
):
    grads = [sg_ref[0, h] for h in range(heads)]
    for n in reversed(range(blocks)):
        span = pl.ds(n * SPAN, SPAN)
        sums_col, sums_row, beta_col = token_vectors(g_ref[0, :, span], b_ref[0, :, span])
        columns, rows, betas, constants = [], [], [], []
        for h in range(heads):
            lanes = pl.ds(h * 128, 128)
            g_col, g_row = sums_col[:, h : h + 1], sums_row[h : h + 1, :]
            beta = beta_col[:, h : h + 1]
            growth = jnp.exp(g_col)
            last = g_col[SPAN - 1 : SPAN, :]
            q_scale, q_full, query = unit(q_ref[0, span, lanes])
            k_scale, k_full, key = unit(k_ref[0, span, lanes])
            cot = d_ref[0, span, lanes]
            update = u_ref[0, span, lanes]
            state = mid_ref[n - 1, h] if n > 0 else None
            score = nt(query, key) * ratio_of(g_col, g_row)
            d_update = tn(score, cot) + nn(key.astype(F32) * jnp.exp(last - g_col), grads[h])
            dx = tn(t_ref[n, h], d_update)
            slope = beta * dx
            dv_ref[0, span, lanes] = slope.astype(BF16)
            d_query, d_key, d_beta, column, row, constant, _ = finish(
                query, key, state, None, beta, g_col, g_row,
                v_ref[0, span, lanes].astype(F32), update, cot, dx, grads[h],
            )
            if n > 0:
                right = jnp.concatenate(
                    [(growth * cot.astype(F32)).astype(BF16), (-growth * slope).astype(BF16)], axis=0
                )
                pair = jnp.concatenate([query, key], axis=0)
                grads[h] = jnp.exp(last) * grads[h] + tn(pair, right)
            dq_ref[0, span, lanes] = unit_back(q_scale, q_full, d_query)
            dk_ref[0, span, lanes] = unit_back(k_scale, k_full, d_key)
            columns.append(column)
            rows.append(row)
            betas.append(d_beta)
            constants.append(constant)
        d_decay, d_beta = token_rows(columns, rows, betas)
        dg_ref[0, :, span] = d_decay + jnp.concatenate(constants, axis=0)
        db_ref[0, :, span] = d_beta


def whole(shape):
    zeros = (0,) * len(shape)
    return pl.BlockSpec(shape, lambda *_: zeros)


def by_row(shape):
    zeros = (0,) * (len(shape) - 1)
    return pl.BlockSpec((1,) + tuple(shape[1:]), lambda j, *_: (j,) + zeros)


def struct(shape, kind):
    return jax.ShapeDtypeStruct(tuple(shape), kind)


def params():
    return pltpu.CompilerParams(vmem_limit_bytes=VMEM_BYTES)


def cost(flops, moved):
    return pl.CostEstimate(flops=flops, bytes_accessed=moved, transcendentals=0)


def on_device(
    prefix_query,
    prefix_key,
    prefix_value,
    prefix_decay,
    prefix_beta,
    prefix_cotangent,
    branch_query,
    branch_key,
    branch_value,
    branch_decay,
    branch_beta,
    branch_cotangent,
    fanout,
    placement,
):
    heads = prefix_decay.shape[1]
    length = prefix_query.shape[1]
    blocks = length // SPAN
    branches = branch_query.shape[0]
    prefixes = fanout.shape[0]
    upto = jnp.arange(prefixes)[:, None] >= jnp.arange(prefixes)[None, :]
    bounds = jnp.sum(jnp.where(upto, fanout[None, :], 0), axis=1)
    parent = jnp.sum((bounds[None, :] <= placement[:, None]).astype(jnp.int32), axis=1)
    unit_flops = 2 * 128 * 128 * 128

    pq, tq = prefix_query.shape, prefix_decay.shape
    prefix_state, mids, updates, prefix_inv = pl.pallas_call(
        functools.partial(prefix_forward_kernel, heads, blocks),
        out_shape=(
            struct((1, heads, 128, 128), F32),
            struct((max(blocks - 1, 1), heads, 128, 128), F32),
            struct(pq, BF16),
            struct((blocks, heads, SPAN, SPAN), BF16),
        ),
        compiler_params=params(),
        cost_estimate=cost(60 * heads * blocks * unit_flops, 10**6),
        name="prefix_forward",
    )(prefix_key, prefix_value, prefix_decay, prefix_beta)
    all_states = lax.all_gather(prefix_state, "pre", axis=0, tiled=True)

    bq, tb = branch_query.shape, branch_decay.shape
    inv_shape = (branches, heads, SPAN, SPAN)
    sums_shape = (prefixes, heads, 128, 128)
    partial_sums, branch_inv, branch_dx, limb_value = pl.pallas_call(
        functools.partial(branch_pull_kernel, heads),
        grid_spec=pltpu.PrefetchScalarGridSpec(
            num_scalar_prefetch=1,
            grid=(branches,),
            in_specs=[by_row(bq), by_row(bq), by_row(bq), by_row(tb), by_row(tb)],
            out_specs=[whole(sums_shape), by_row(inv_shape), by_row(bq), by_row(bq)],
        ),
        out_shape=(
            struct(sums_shape, F32),
            struct(inv_shape, BF16),
            struct(bq, BF16),
            struct(bq, BF16),
        ),
        compiler_params=params(),
        cost_estimate=cost(80 * heads * branches * unit_flops, 5 * 10**6),
        name="branch_pull",
    )(parent, branch_query, branch_key, branch_cotangent, branch_decay, branch_beta)
    state_grad = lax.psum_scatter(partial_sums, "pre", scatter_dimension=0, tiled=True)

    branch_out, limb_query, limb_key, limb_decay, limb_beta = pl.pallas_call(
        functools.partial(branch_finish_kernel, heads),
        grid_spec=pltpu.PrefetchScalarGridSpec(
            num_scalar_prefetch=1,
            grid=(branches,),
            in_specs=[
                by_row(bq), by_row(bq), by_row(bq), by_row(bq), by_row(tb), by_row(tb),
                by_row(inv_shape), by_row(bq),
                pl.BlockSpec((1, heads, 128, 128), lambda j, parent: (parent[j], 0, 0, 0)),
            ],
            out_specs=[by_row(bq), by_row(bq), by_row(bq), by_row(tb), by_row(tb)],
        ),
        out_shape=(
            struct(bq, BF16), struct(bq, BF16), struct(bq, BF16), struct(tb, F32), struct(tb, F32),
        ),
        compiler_params=params(),
        cost_estimate=cost(80 * heads * branches * unit_flops, 5 * 10**6),
        name="branch_finish",
    )(
        parent, branch_query, branch_key, branch_value, branch_cotangent, branch_decay,
        branch_beta, branch_inv, branch_dx, all_states,
    )

    trunk_query, trunk_key, trunk_value, trunk_decay, trunk_beta = pl.pallas_call(
        functools.partial(prefix_finish_kernel, heads, blocks),
        out_shape=(
            struct(pq, BF16), struct(pq, BF16), struct(pq, BF16), struct(tq, F32), struct(tq, F32),
        ),
        compiler_params=params(),
        cost_estimate=cost(60 * heads * blocks * unit_flops, 2 * 10**6),
        name="prefix_finish",
    )(
        prefix_query, prefix_key, prefix_value, prefix_cotangent, prefix_decay, prefix_beta,
        prefix_inv, updates, mids, state_grad,
    )
    return (
        branch_out,
        trunk_query,
        trunk_key,
        trunk_value,
        trunk_decay,
        trunk_beta,
        limb_query,
        limb_key,
        limb_value,
        limb_decay,
        limb_beta,
    )


def solution(mesh):
    data = P(("group", "pre"), None, ("head", "sub"))
    token = P(("group", "pre"), ("head", "sub"), None)
    in_specs = (
        data, data, data, token, token, data,
        data, data, data, token, token, data,
        P("group"), P(("group", "pre")),
    )
    out_specs = (data, data, data, data, token, token, data, data, data, token, token)
    return jax.shard_map(
        on_device, mesh=mesh, in_specs=in_specs, out_specs=out_specs, check_vma=False
    )
```

profile of v0, /device:TPU:0, one launch (start us, length us, event | category | flops | bytes accessed | tf_op | source)
XLA Modules:
  0.0 92.8 jit_solution(6972441845179750317)
XLA Ops:
  7.2 0.0 copy-start.1
  7.2 0.0 copy-start.2
  7.2 0.0 copy-start.4
  7.2 0.0 all-gather.2.cloned.1.call-start
  7.3 0.0 copy-start.5
  7.3 1.0 %copy-done.5 = bf16[1,256,512]{2,1,0:T(8,128)(2,1)S(1)} copy-done((bf16[1,256,512]{2,1,0:T(8,128)(2,1)S(1)}, bf16[1,256,512]{2,1,0:T(8,128)(2,1)}, u32[]{:S(2)}) %copy-start.5) | copy-done | bytes 262168
  8.3 0.0 copy-start.7
  8.3 0.9 %copy-done.7 = bf16[1,256,512]{2,1,0:T(8,128)(2,1)S(1)} copy-done((bf16[1,256,512]{2,1,0:T(8,128)(2,1)S(1)}, bf16[1,256,512]{2,1,0:T(8,128)(2,1)}, u32[]{:S(2)}) %copy-start.7) | copy-done | bytes 262168
  9.3 0.7 copy-done.14
  10.0 0.7 copy-done.16
  10.6 4.0 %prefix_forward.1 = (f32[1,4,128,128]{3,2,1,0:T(8,128)}, f32[1,4,128,128]{3,2,1,0:T(8,128)S(1)}, bf16[1,256,512]{2,1,0:T(8,128)(2,1)S(1)}, bf16[2,4,128,128]{3,2,1,0:T(8,128)(2,1)S(1)}) custom-call(bf16[1,256,512]{2,1,0:T(8,128)(2,1)S(1)} %copy-done.5, bf16[1,256,512]{2,1,0:T(8,128)(2,1)S(1)} %copy-done.7, f32[1,4,256]{2,1,0:T(4,128)S(1)} %copy-done.14, ...), custom_call_target="tpu_custom_call" | custom-call | flops 2013265920 | bytes 1000000 | tf_op jit(solution)/shard_map/prefix_forward/pallas_call | solution.py:347
  14.6 0.7 copy-done.18
  15.3 0.0 all-gather.2.cloned.1.call-update
  15.4 0.0 copy-start.27
  15.4 0.2 reduce-scatter.2.cloned.1.call-start
  15.6 0.4 copy-done.26
  16.0 0.1 select_reduce_fusion
  16.1 0.0 copy-done.27
  16.1 0.2 convert_reduce_fusion.parent_ref
  16.3 0.0 copy-done.1
  16.3 0.0 copy-done.2
  16.3 0.0 copy-done.4
  16.3 0.0 copy-done.12
  16.3 0.0 copy-done.13
  16.4 11.4 %branch_pull.1 = (f32[4,4,128,128]{3,2,1,0:T(8,128)}, bf16[4,4,128,128]{3,2,1,0:T(8,128)(2,1)S(1)}, bf16[4,128,512]{2,1,0:T(8,128)(2,1)S(1)}, bf16[4,128,512]{2,1,0:T(8,128)(2,1)}) custom-call(s32[4]{0:T(128)S(1)} %convert_reduce_fusion.parent_ref, bf16[4,128,512]{2,1,0:T(8,128)(2,1)S(1)} %copy-done.1, bf16[4,128,512]{2,1,0:T(8,128)(2,1)S(1)} %copy-done.2, ...), custom_call_target="tpu_custom_call" | custom-call | flops 5368709120 | bytes 5000000 | tf_op jit(solution)/shard_map/branch_pull/pallas_call | solution.py:364
  27.7 0.0 copy-done.20
  27.7 0.8 copy-done.22
  28.5 0.0 reduce-scatter.2.cloned.1.call-update
  28.6 0.8 copy-done.24
  29.3 16.8 %all-gather.2.cloned.1.call-done.s_ref = f32[4,4,128,128]{3,2,1,0:T(8,128)} async-done(((f32[1,4,128,128]{3,2,1,0:T(8,128)}), f32[4,4,128,128]{3,2,1,0:T(8,128)}) %all-gather.2.cloned.1.call-update) | async-done | bytes 1048592 | tf_op jit(solution)/shard_map/all_gather | solution.py:359
  46.1 0.0 copy-done.3
  46.1 1.2 %copy-done = f32[4,4,128,128]{3,2,1,0:T(8,128)S(1)} copy-done((f32[4,4,128,128]{3,2,1,0:T(8,128)S(1)}, f32[4,4,128,128]{3,2,1,0:T(8,128)}, u32[]{:S(2)}) %copy-start) | copy-done | bytes 1048600
  47.4 1.0 %copy-done.23 = bf16[4,4,128,128]{3,2,1,0:T(8,128)(2,1)S(1)} copy-done((bf16[4,4,128,128]{3,2,1,0:T(8,128)(2,1)S(1)}, bf16[4,4,128,128]{3,2,1,0:T(8,128)(2,1)}, u32[]{:S(2)}) %copy-start.23) | copy-done | bytes 524312
  48.4 1.0 %copy-done.25 = bf16[4,128,512]{2,1,0:T(8,128)(2,1)S(1)} copy-done((bf16[4,128,512]{2,1,0:T(8,128)(2,1)S(1)}, bf16[4,128,512]{2,1,0:T(8,128)(2,1)}, u32[]{:S(2)}) %copy-start.25) | copy-done | bytes 524312
  49.5 0.0 copy-start.17
  49.5 11.3 %branch_finish.1 = (bf16[4,128,512]{2,1,0:T(8,128)(2,1)}, bf16[4,128,512]{2,1,0:T(8,128)(2,1)}, bf16[4,128,512]{2,1,0:T(8,128)(2,1)}, f32[4,4,128]{2,1,0:T(4,128)}, f32[4,4,128]{2,1,0:T(4,128)}) custom-call(s32[4]{0:T(128)S(1)} %convert_reduce_fusion.parent_ref, bf16[4,128,512]{2,1,0:T(8,128)(2,1)S(1)} %copy-done.1, bf16[4,128,512]{2,1,0:T(8,128)(2,1)S(1)} %copy-done.2, ...), custom_call_target="tpu_custom_call" | custom-call | flops 5368709120 | bytes 5000000 | tf_op jit(solution)/shard_map/branch_finish/pallas_call | solution.py:384
  60.7 14.4 %reduce-scatter.2.cloned.1.call-done.sg_ref = f32[1,4,128,128]{3,2,1,0:T(8,128)} async-done(((f32[4,4,128,128]{3,2,1,0:T(8,128)}), f32[1,4,128,128]{3,2,1,0:T(8,128)}) %reduce-scatter.2.cloned.1.call-update) | async-done | bytes 262160 | tf_op jit(solution)/shard_map/reduce_scatter | solution.py:382
  75.1 0.0 copy-done.6
  75.1 0.0 copy-done.8
  75.1 0.0 copy-done.9
  75.1 0.0 copy-done.10
  75.1 0.0 copy-done.17
  75.1 0.0 copy-done.15
  75.2 0.0 copy-start.11
  75.2 0.9 %copy-done.11 = f32[1,4,128,128]{3,2,1,0:T(8,128)S(1)} copy-done((f32[1,4,128,128]{3,2,1,0:T(8,128)S(1)}, f32[1,4,128,128]{3,2,1,0:T(8,128)}, u32[]{:S(2)}) %copy-start.11) | copy-done | bytes 262168
  76.1 0.9 %copy-done.19 = bf16[1,256,512]{2,1,0:T(8,128)(2,1)S(1)} copy-done((bf16[1,256,512]{2,1,0:T(8,128)(2,1)S(1)}, bf16[1,256,512]{2,1,0:T(8,128)(2,1)}, u32[]{:S(2)}) %copy-start.19) | copy-done | bytes 262168
  77.1 0.9 %copy-done.21 = bf16[2,4,128,128]{3,2,1,0:T(8,128)(2,1)S(1)} copy-done((bf16[2,4,128,128]{3,2,1,0:T(8,128)(2,1)S(1)}, bf16[2,4,128,128]{3,2,1,0:T(8,128)(2,1)}, u32[]{:S(2)}) %copy-start.21) | copy-done | bytes 262168
  78.0 7.9 %prefix_finish.1 = (bf16[1,256,512]{2,1,0:T(8,128)(2,1)}, bf16[1,256,512]{2,1,0:T(8,128)(2,1)}, bf16[1,256,512]{2,1,0:T(8,128)(2,1)}, f32[1,4,256]{2,1,0:T(4,128)}, f32[1,4,256]{2,1,0:T(4,128)}) custom-call(bf16[1,256,512]{2,1,0:T(8,128)(2,1)S(1)} %copy-done.9, bf16[1,256,512]{2,1,0:T(8,128)(2,1)S(1)} %copy-done.6, bf16[1,256,512]{2,1,0:T(8,128)(2,1)S(1)} %copy-done.8, ...), custom_call_target="tpu_custom_call" | custom-call | flops 2013265920 | bytes 2000000 | tf_op jit(solution)/shard_map/prefix_finish/pallas_call | solution.py:407
  (20 shorter events, 0.0 us)
Async XLA Ops:
  7.2 9.1 %copy-start.1 = (bf16[4,128,512]{2,1,0:T(8,128)(2,1)S(1)}, bf16[4,128,512]{2,1,0:T(8,128)(2,1)}, u32[]{:S(2)}) copy-start(bf16[4,128,512]{2,1,0:T(8,128)(2,1)} %q_ref.4) | copy-start | bytes 1572868
  7.2 9.1 %copy-start.2 = (bf16[4,128,512]{2,1,0:T(8,128)(2,1)S(1)}, bf16[4,128,512]{2,1,0:T(8,128)(2,1)}, u32[]{:S(2)}) copy-start(bf16[4,128,512]{2,1,0:T(8,128)(2,1)} %k_ref.6) | copy-start | bytes 1572868
  7.2 9.1 %copy-start.4 = (bf16[4,128,512]{2,1,0:T(8,128)(2,1)S(1)}, bf16[4,128,512]{2,1,0:T(8,128)(2,1)}, u32[]{:S(2)}) copy-start(bf16[4,128,512]{2,1,0:T(8,128)(2,1)} %d_ref.4) | copy-start | bytes 1572868
  7.2 38.9 %all-gather.2.cloned.1.call-start = ((), (), s32[]{:S(2)}) async-start(), calls=%async_computation.1 | async-start | bytes 1310720 | tf_op jit(solution)/shard_map/all_gather | solution.py:359
  7.3 1.1 %copy-start.5 = (bf16[1,256,512]{2,1,0:T(8,128)(2,1)S(1)}, bf16[1,256,512]{2,1,0:T(8,128)(2,1)}, u32[]{:S(2)}) copy-start(bf16[1,256,512]{2,1,0:T(8,128)(2,1)} %k_ref.7) | copy-start | bytes 786436
  8.3 0.9 %copy-start.7 = (bf16[1,256,512]{2,1,0:T(8,128)(2,1)S(1)}, bf16[1,256,512]{2,1,0:T(8,128)(2,1)}, u32[]{:S(2)}) copy-start(bf16[1,256,512]{2,1,0:T(8,128)(2,1)} %v_ref.5) | copy-start | bytes 786436
  9.3 0.7 copy-start.14
  9.9 0.7 copy-start.16
  14.6 0.7 copy-start.18
  15.3 12.4 %copy-start.20 = (bf16[2,4,128,128]{3,2,1,0:T(8,128)(2,1)}, bf16[2,4,128,128]{3,2,1,0:T(8,128)(2,1)S(1)}, u32[]{:S(2)}) copy-start(bf16[2,4,128,128]{3,2,1,0:T(8,128)(2,1)S(1)} %get-tuple-element.33.t_ref) | copy-start | bytes 786436
  15.3 0.7 copy-start.26
  15.3 1.0 %copy-start.12 = (f32[4,4,128]{2,1,0:T(4,128)S(1)}, f32[4,4,128]{2,1,0:T(4,128)}, u32[]{:S(2)}) copy-start(f32[4,4,128]{2,1,0:T(4,128)} %g_ref.6) | copy-start | bytes 24580
  15.3 1.0 %copy-start.13 = (f32[4,4,128]{2,1,0:T(4,128)S(1)}, f32[4,4,128]{2,1,0:T(4,128)}, u32[]{:S(2)}) copy-start(f32[4,4,128]{2,1,0:T(4,128)} %b_ref.6) | copy-start | bytes 24580
  15.4 0.8 copy-start.27
  15.4 59.7 %reduce-scatter.2.cloned.1.call-start = ((), (), s32[]{:S(2)}) async-start(), calls=%async_computation.2 | async-start | bytes 1310720 | tf_op jit(solution)/shard_map/reduce_scatter | solution.py:382
  27.7 0.8 copy-start.22
  28.5 0.8 copy-start.24
  28.5 17.6 %copy-start.3 = (bf16[4,128,512]{2,1,0:T(8,128)(2,1)S(1)}, bf16[4,128,512]{2,1,0:T(8,128)(2,1)}, u32[]{:S(2)}) copy-start(bf16[4,128,512]{2,1,0:T(8,128)(2,1)} %v_ref.4) | copy-start | bytes 1572868
  46.1 1.2 %copy-start = (f32[4,4,128,128]{3,2,1,0:T(8,128)S(1)}, f32[4,4,128,128]{3,2,1,0:T(8,128)}, u32[]{:S(2)}) copy-start(f32[4,4,128,128]{3,2,1,0:T(8,128)} %all-gather.2.cloned.1.call-done.s_ref) | copy-start | bytes 3145732
  47.4 1.0 %copy-start.23 = (bf16[4,4,128,128]{3,2,1,0:T(8,128)(2,1)S(1)}, bf16[4,4,128,128]{3,2,1,0:T(8,128)(2,1)}, u32[]{:S(2)}) copy-start(bf16[4,4,128,128]{3,2,1,0:T(8,128)(2,1)} %copy-done.22) | copy-start | bytes 1572868
  48.4 1.0 %copy-start.25 = (bf16[4,128,512]{2,1,0:T(8,128)(2,1)S(1)}, bf16[4,128,512]{2,1,0:T(8,128)(2,1)}, u32[]{:S(2)}) copy-start(bf16[4,128,512]{2,1,0:T(8,128)(2,1)} %copy-done.24) | copy-start | bytes 1572868
  49.4 25.7 %copy-start.6 = (bf16[1,256,512]{2,1,0:T(8,128)(2,1)S(1)}, bf16[1,256,512]{2,1,0:T(8,128)(2,1)}, u32[]{:S(2)}) copy-start(bf16[1,256,512]{2,1,0:T(8,128)(2,1)} %k_ref.7) | copy-start | bytes 786436
  49.4 25.7 %copy-start.8 = (bf16[1,256,512]{2,1,0:T(8,128)(2,1)S(1)}, bf16[1,256,512]{2,1,0:T(8,128)(2,1)}, u32[]{:S(2)}) copy-start(bf16[1,256,512]{2,1,0:T(8,128)(2,1)} %v_ref.5) | copy-start | bytes 786436
  49.4 25.7 %copy-start.9 = (bf16[1,256,512]{2,1,0:T(8,128)(2,1)S(1)}, bf16[1,256,512]{2,1,0:T(8,128)(2,1)}, u32[]{:S(2)}) copy-start(bf16[1,256,512]{2,1,0:T(8,128)(2,1)} %q_ref.5) | copy-start | bytes 786436
  49.5 25.7 %copy-start.10 = (bf16[1,256,512]{2,1,0:T(8,128)(2,1)S(1)}, bf16[1,256,512]{2,1,0:T(8,128)(2,1)}, u32[]{:S(2)}) copy-start(bf16[1,256,512]{2,1,0:T(8,128)(2,1)} %d_ref.5) | copy-start | bytes 786436
  49.5 25.7 %copy-start.17 = (f32[1,4,256]{2,1,0:T(4,128)S(1)}, f32[1,4,256]{2,1,0:T(4,128)}, u32[]{:S(2)}) copy-start(f32[1,4,256]{2,1,0:T(4,128)} %b_ref.7) | copy-start | bytes 12292
  60.7 14.4 %copy-start.15 = (f32[1,4,256]{2,1,0:T(4,128)S(1)}, f32[1,4,256]{2,1,0:T(4,128)}, u32[]{:S(2)}) copy-start(f32[1,4,256]{2,1,0:T(4,128)} %g_ref.7) | copy-start | bytes 12292
  75.2 1.0 %copy-start.11 = (f32[1,4,128,128]{3,2,1,0:T(8,128)S(1)}, f32[1,4,128,128]{3,2,1,0:T(8,128)}, u32[]{:S(2)}) copy-start(f32[1,4,128,128]{3,2,1,0:T(8,128)} %reduce-scatter.2.cloned.1.call-done.sg_ref) | copy-start | bytes 786436
  76.1 0.9 %copy-start.19 = (bf16[1,256,512]{2,1,0:T(8,128)(2,1)S(1)}, bf16[1,256,512]{2,1,0:T(8,128)(2,1)}, u32[]{:S(2)}) copy-start(bf16[1,256,512]{2,1,0:T(8,128)(2,1)} %copy-done.18) | copy-start | bytes 786436
  77.1 0.9 %copy-start.21 = (bf16[2,4,128,128]{3,2,1,0:T(8,128)(2,1)S(1)}, bf16[2,4,128,128]{3,2,1,0:T(8,128)(2,1)}, u32[]{:S(2)}) copy-start(bf16[2,4,128,128]{3,2,1,0:T(8,128)(2,1)} %copy-done.20) | copy-start | bytes 786436
Sparse Core Ops, SparseCore 0:
  15.5 30.5 all-gather.1
  48.4 26.6 reduce-scatter.1
where the time goes:
time: 93.3 us; the launch traced here: 92.8 us
  Pallas kernels  34.6 us (37%)
  waiting for transfers between devices  31.2 us (33%)
  between operations  14.2 us (15%)
  local copies, waits for them, and re-layouts  12.2 us (13%)
    all_gather x1, waiting for transfers between devices, on_device(): all_states = lax.all_gather(prefix_state, 'pre', axis=0, tiled=True)  16.8 us
    reduce_scatter x1, waiting for transfers between devices, on_device(): lax.psum_scatter(partial_sums, 'pre', scatter_dimension=0, tiled=True)  14.4 us
    unnamed x56, local copies, waits for them, and re-layouts  12.2 us
    pallas_call x1, Pallas kernels, on_device(): pl.pallas_call(functools.partial(branch_pull_kernel, heads), grid_spec=pl...  11.4 us
    pallas_call x1, Pallas kernels, on_device(): pl.pallas_call(functools.partial(branch_finish_kernel, heads), grid_spec=...  11.3 us
    pallas_call x1, Pallas kernels, on_device(): pl.pallas_call(functools.partial(prefix_finish_kernel, heads, blocks), ou...  7.93 us
    pallas_call x1, Pallas kernels, on_device(): pl.pallas_call(functools.partial(prefix_forward_kernel, heads, blocks), o...  3.99 us
  transfers between devices with their start and end apart: 2, of which 2 were waited for; matrix products, arithmetic and copies ran while one was open for 0% of the time, Pallas kernels for 24%

commit v1 on v0

--- a/solution.py
+++ b/solution.py
@@ -317,6 +317,10 @@
     return pl.CostEstimate(flops=flops, bytes_accessed=moved, transcendentals=0)
 
 
+def shifted(x, steps, count):
+    return lax.ppermute(x, "pre", [(i, (i + steps) % count) for i in range(count)])
+
+
 def on_device(
     prefix_query,
     prefix_key,
@@ -341,6 +345,9 @@
     upto = jnp.arange(prefixes)[:, None] >= jnp.arange(prefixes)[None, :]
     bounds = jnp.sum(jnp.where(upto, fanout[None, :], 0), axis=1)
     parent = jnp.sum((bounds[None, :] <= placement[:, None]).astype(jnp.int32), axis=1)
+    place = lax.axis_index("pre")
+    send_slot = lax.rem(parent - place + prefixes, prefixes)
+    state_slot = lax.rem(place - parent + prefixes, prefixes)
     unit_flops = 2 * 128 * 128 * 128
 
     pq, tq = prefix_query.shape, prefix_decay.shape
@@ -356,7 +363,9 @@
         cost_estimate=cost(60 * heads * blocks * unit_flops, 10**6),
         name="prefix_forward",
     )(prefix_key, prefix_value, prefix_decay, prefix_beta)
-    all_states = lax.all_gather(prefix_state, "pre", axis=0, tiled=True)
+    all_states = jnp.concatenate(
+        [prefix_state] + [shifted(prefix_state, n, prefixes) for n in range(1, prefixes)], axis=0
+    )
 
     bq, tb = branch_query.shape, branch_decay.shape
     inv_shape = (branches, heads, SPAN, SPAN)
@@ -378,8 +387,10 @@
         compiler_params=params(),
         cost_estimate=cost(80 * heads * branches * unit_flops, 5 * 10**6),
         name="branch_pull",
-    )(parent, branch_query, branch_key, branch_cotangent, branch_decay, branch_beta)
-    state_grad = lax.psum_scatter(partial_sums, "pre", scatter_dimension=0, tiled=True)
+    )(send_slot, branch_query, branch_key, branch_cotangent, branch_decay, branch_beta)
+    state_grad = partial_sums[:1]
+    for n in range(1, prefixes):
+        state_grad = state_grad + shifted(partial_sums[n : n + 1], n, prefixes)
 
     branch_out, limb_query, limb_key, limb_decay, limb_beta = pl.pallas_call(
         functools.partial(branch_finish_kernel, heads),
@@ -400,7 +411,7 @@
         cost_estimate=cost(80 * heads * branches * unit_flops, 5 * 10**6),
         name="branch_finish",
     )(
-        parent, branch_query, branch_key, branch_value, branch_cotangent, branch_decay,
+        state_slot, branch_query, branch_key, branch_value, branch_cotangent, branch_decay,
         branch_beta, branch_inv, branch_dx, all_states,
     )
 

time: 93.3 us -> 65.4 us (0.70)
  the two profiles are of different devices: /device:TPU:0 before, /device:TPU:28 now
where the time goes in v1:
time: 65.4 us; the launch traced here: 65.2 us
  Pallas kernels  33.4 us (51%)
  waiting for transfers between devices  16.3 us (25%)
  starting transfers between devices  9.62 us (15%)
  local copies, waits for them, and re-layouts  4.52 us (7%)
  between operations  0.84 us (1%)
    ppermute x6, waiting for transfers between devices, shifted(): lax.ppermute(x, 'pre', [(i, (i + steps) % count) for i in range(count)])  16.3 us
    pallas_call x1, Pallas kernels, on_device(): pl.pallas_call(functools.partial(branch_finish_kernel, heads), grid_spec=...  11.3 us
    pallas_call x1, Pallas kernels, on_device(): pl.pallas_call(functools.partial(branch_pull_kernel, heads), grid_spec=pl...  10.9 us
    ppermute x6, starting transfers between devices, shifted(): lax.ppermute(x, 'pre', [(i, (i + steps) % count) for i in range(count)])  9.62 us
    pallas_call x1, Pallas kernels, on_device(): pl.pallas_call(functools.partial(prefix_finish_kernel, heads, blocks), ou...  7.94 us
    unnamed x36, local copies, waits for them, and re-layouts  4.46 us
    pallas_call x1, Pallas kernels, on_device(): pl.pallas_call(functools.partial(prefix_forward_kernel, heads, blocks), o...  3.28 us
  transfers between devices with their start and end apart: 6, of which 1 were waited for; matrix products, arithmetic and copies ran while one was open for 1% of the time, Pallas kernels for 34%

profile of v1, /device:TPU:28, one launch (start us, length us, event | category | flops | bytes accessed | tf_op | source)
XLA Modules:
  0.0 65.2 jit_solution(6936651294972938391)
XLA Ops:
  0.6 0.0 copy-start
  0.7 0.0 copy-start.1
  0.7 0.0 copy-start.3
  0.7 0.0 copy-start.4
  0.7 1.1 %copy-done.4 = bf16[1,256,512]{2,1,0:T(8,128)(2,1)S(1)} copy-done((bf16[1,256,512]{2,1,0:T(8,128)(2,1)S(1)}, bf16[1,256,512]{2,1,0:T(8,128)(2,1)}, u32[]{:S(2)}) %copy-start.4) | copy-done | bytes 262168
  1.7 0.9 %copy-done.6 = bf16[1,256,512]{2,1,0:T(8,128)(2,1)S(1)} copy-done((bf16[1,256,512]{2,1,0:T(8,128)(2,1)S(1)}, bf16[1,256,512]{2,1,0:T(8,128)(2,1)}, u32[]{:S(2)}) %copy-start.6) | copy-done | bytes 262168
  2.7 0.7 %copy-done.12 = f32[1,4,256]{2,1,0:T(4,128)S(1)} copy-done((f32[1,4,256]{2,1,0:T(4,128)S(1)}, f32[1,4,256]{2,1,0:T(4,128)}, u32[]{:S(2)}) %copy-start.12) | copy-done | bytes 4120
  3.4 0.7 %copy-done.14 = f32[1,4,256]{2,1,0:T(4,128)S(1)} copy-done((f32[1,4,256]{2,1,0:T(4,128)S(1)}, f32[1,4,256]{2,1,0:T(4,128)}, u32[]{:S(2)}) %copy-start.14) | copy-done | bytes 4120
  4.1 3.3 %prefix_forward.1 = (f32[1,4,128,128]{3,2,1,0:T(8,128)S(1)}, f32[1,4,128,128]{3,2,1,0:T(8,128)S(1)}, bf16[1,256,512]{2,1,0:T(8,128)(2,1)S(1)}, bf16[2,4,128,128]{3,2,1,0:T(8,128)(2,1)S(1)}) custom-call(bf16[1,256,512]{2,1,0:T(8,128)(2,1)S(1)} %copy-done.4, bf16[1,256,512]{2,1,0:T(8,128)(2,1)S(1)} %copy-done.6, f32[1,4,256]{2,1,0:T(4,128)S(1)} %copy-done.12, ...), custom_call_target="tpu_custom_call" | custom-call | flops 2013265920 | bytes 1000000 | tf_op jit(solution)/shard_map/prefix_forward/pallas_call | solution.py:354
  7.4 0.0 copy-start.11
  7.4 0.0 copy-start.10
  7.4 0.3 collective-permute-start
  7.7 1.7 %collective-permute-start.1 = (f32[1,4,128,128]{3,2,1,0:T(8,128)S(1)}, f32[1,4,128,128]{3,2,1,0:T(8,128)S(1)}, u32[]{:S(2)}, u32[]{:S(2)}) collective-permute-start(f32[1,4,128,128]{3,2,1,0:T(8,128)S(1)} %get-tuple-element.31), channel_id=1, source_target_pairs={{0,8},{4,12},{8,0},{12,4},{1,9},{5,13},{9,1},{13,5},{2,10},{6,14},... | collective-permute-start | bytes 786440 | tf_op jit(solution)/shard_map/ppermute | solution.py:321
  9.4 0.4 collective-permute-start.2
  9.8 0.0 copy-done.16
  9.8 0.1 select_reduce_fusion
  9.9 0.0 copy-done.17
  9.9 0.2 convert_reduce_fusion
  10.1 0.0 copy-done
  10.1 0.0 copy-done.1
  10.1 0.0 copy-done.3
  10.1 0.0 copy-done.11
  10.2 0.0 copy-done.10
  10.2 10.9 %branch_pull.1 = (f32[4,4,128,128]{3,2,1,0:T(8,128)S(1)}, bf16[4,4,128,128]{3,2,1,0:T(8,128)(2,1)S(1)}, bf16[4,128,512]{2,1,0:T(8,128)(2,1)S(1)}, bf16[4,128,512]{2,1,0:T(8,128)(2,1)}) custom-call(s32[4]{0:T(128)S(1)} %get-tuple-element.50.parent_ref, bf16[4,128,512]{2,1,0:T(8,128)(2,1)S(1)} %copy-done, bf16[4,128,512]{2,1,0:T(8,128)(2,1)S(1)} %copy-done.1, ...), custom_call_target="tpu_custom_call" | custom-call | flops 5368709120 | bytes 5000000 | tf_op jit(solution)/shard_map/branch_pull/pallas_call | solution.py:373
  21.1 0.1 fusion.2
  21.2 3.4 %collective-permute-start.3 = (f32[1,4,128,128]{3,2,1,0:T(8,128)S(1)}, f32[1,4,128,128]{3,2,1,0:T(8,128)S(1)}, u32[]{:S(2)}, u32[]{:S(2)}) collective-permute-start(f32[1,4,128,128]{3,2,1,0:T(8,128)S(1)} %get-tuple-element.47), channel_id=1, source_target_pairs={{0,4},{4,8},{8,12},{12,0},{1,5},{5,9},{9,13},{13,1},{2,6},{6,10},{... | collective-permute-start | bytes 786440 | tf_op jit(solution)/shard_map/ppermute | solution.py:321
  24.6 0.0 collective-permute-start.4
  24.6 0.0 collective-permute-done
  24.6 3.8 %collective-permute-start.5 = (f32[1,4,128,128]{3,2,1,0:T(8,128)S(1)}, f32[1,4,128,128]{3,2,1,0:T(8,128)S(1)}, u32[]{:S(2)}, u32[]{:S(2)}) collective-permute-start(f32[1,4,128,128]{3,2,1,0:T(8,128)S(1)} %get-tuple-element.48), channel_id=1, source_target_pairs={{0,12},{4,0},{8,4},{12,8},{1,13},{5,1},{9,5},{13,9},{2,14},{6,2},{... | collective-permute-start | bytes 786440 | tf_op jit(solution)/shard_map/ppermute | solution.py:321
  28.4 16.3 %collective-permute-done.1 = f32[1,4,128,128]{3,2,1,0:T(8,128)S(1)} collective-permute-done((f32[1,4,128,128]{3,2,1,0:T(8,128)S(1)}, f32[1,4,128,128]{3,2,1,0:T(8,128)S(1)}, u32[]{:S(2)}, u32[]{:S(2)}) %collective-permute-start.1) | collective-permute-done | bytes 262176 | tf_op jit(solution)/shard_map/ppermute | solution.py:321
  44.7 0.0 collective-permute-done.2
  44.7 0.1 pad_maximum_fusion.s_ref
  44.7 0.0 copy-done.2
  44.7 11.3 %branch_finish.1 = (bf16[4,128,512]{2,1,0:T(8,128)(2,1)}, bf16[4,128,512]{2,1,0:T(8,128)(2,1)}, bf16[4,128,512]{2,1,0:T(8,128)(2,1)}, f32[4,4,128]{2,1,0:T(4,128)}, f32[4,4,128]{2,1,0:T(4,128)}) custom-call(s32[4]{0:T(128)S(1)} %get-tuple-element.51.parent_ref, bf16[4,128,512]{2,1,0:T(8,128)(2,1)S(1)} %copy-done, bf16[4,128,512]{2,1,0:T(8,128)(2,1)S(1)} %copy-done.1, ...), custom_call_target="tpu_custom_call" | custom-call | flops 5368709120 | bytes 5000000 | tf_op jit(solution)/shard_map/branch_finish/pallas_call | solution.py:395
  56.0 0.0 copy-start.8
  56.1 0.0 copy-start.9
  56.1 0.0 collective-permute-done.3
  56.1 0.0 collective-permute-done.4
  56.1 0.0 collective-permute-done.5
  56.1 0.0 copy-start.15
  56.1 0.1 add_add_fusion.sg_ref
  56.2 0.0 copy-start.13
  56.2 0.8 %copy-done.5 = bf16[1,256,512]{2,1,0:T(8,128)(2,1)S(1)} copy-done((bf16[1,256,512]{2,1,0:T(8,128)(2,1)S(1)}, bf16[1,256,512]{2,1,0:T(8,128)(2,1)}, u32[]{:S(2)}) %copy-start.5) | copy-done | bytes 262168
  57.0 0.1 copy-done.7
  57.1 0.1 copy-done.8
  57.2 0.1 copy-done.9
  57.2 0.0 copy-done.15
  57.2 7.9 %prefix_finish.1 = (bf16[1,256,512]{2,1,0:T(8,128)(2,1)}, bf16[1,256,512]{2,1,0:T(8,128)(2,1)}, bf16[1,256,512]{2,1,0:T(8,128)(2,1)}, f32[1,4,256]{2,1,0:T(4,128)}, f32[1,4,256]{2,1,0:T(4,128)}) custom-call(bf16[1,256,512]{2,1,0:T(8,128)(2,1)S(1)} %copy-done.8, bf16[1,256,512]{2,1,0:T(8,128)(2,1)S(1)} %copy-done.5, bf16[1,256,512]{2,1,0:T(8,128)(2,1)S(1)} %copy-done.7, ...), custom_call_target="tpu_custom_call" | custom-call | flops 2013265920 | bytes 2000000 | tf_op jit(solution)/shard_map/prefix_finish/pallas_call | solution.py:418
  (10 shorter events, 0.0 us)
Async XLA Ops:
  0.6 9.5 %copy-start = (bf16[4,128,512]{2,1,0:T(8,128)(2,1)S(1)}, bf16[4,128,512]{2,1,0:T(8,128)(2,1)}, u32[]{:S(2)}) copy-start(bf16[4,128,512]{2,1,0:T(8,128)(2,1)} %q_ref.4) | copy-start | bytes 1572868
  0.7 9.5 %copy-start.1 = (bf16[4,128,512]{2,1,0:T(8,128)(2,1)S(1)}, bf16[4,128,512]{2,1,0:T(8,128)(2,1)}, u32[]{:S(2)}) copy-start(bf16[4,128,512]{2,1,0:T(8,128)(2,1)} %k_ref.6) | copy-start | bytes 1572868
  0.7 9.5 %copy-start.3 = (bf16[4,128,512]{2,1,0:T(8,128)(2,1)S(1)}, bf16[4,128,512]{2,1,0:T(8,128)(2,1)}, u32[]{:S(2)}) copy-start(bf16[4,128,512]{2,1,0:T(8,128)(2,1)} %d_ref.4) | copy-start | bytes 1572868
  0.7 1.1 %copy-start.4 = (bf16[1,256,512]{2,1,0:T(8,128)(2,1)S(1)}, bf16[1,256,512]{2,1,0:T(8,128)(2,1)}, u32[]{:S(2)}) copy-start(bf16[1,256,512]{2,1,0:T(8,128)(2,1)} %k_ref.7) | copy-start | bytes 786436
  1.7 0.9 %copy-start.6 = (bf16[1,256,512]{2,1,0:T(8,128)(2,1)S(1)}, bf16[1,256,512]{2,1,0:T(8,128)(2,1)}, u32[]{:S(2)}) copy-start(bf16[1,256,512]{2,1,0:T(8,128)(2,1)} %v_ref.5) | copy-start | bytes 786436
  2.7 0.7 %copy-start.12 = (f32[1,4,256]{2,1,0:T(4,128)S(1)}, f32[1,4,256]{2,1,0:T(4,128)}, u32[]{:S(2)}) copy-start(f32[1,4,256]{2,1,0:T(4,128)} %g_ref.7) | copy-start | bytes 12292
  3.4 0.7 %copy-start.14 = (f32[1,4,256]{2,1,0:T(4,128)S(1)}, f32[1,4,256]{2,1,0:T(4,128)}, u32[]{:S(2)}) copy-start(f32[1,4,256]{2,1,0:T(4,128)} %b_ref.7) | copy-start | bytes 12292
  4.1 5.7 %copy-start.16 = (s32[4]{0:T(128)S(1)}, s32[4]{0:T(128)}, u32[]{:S(2)}) copy-start(s32[4]{0:T(128)} %param.26) | copy-start | bytes 52
  4.1 5.9 %copy-start.17 = (s32[4]{0:T(128)S(1)}, s32[4]{0:T(128)}, u32[]{:S(2)}) copy-start(s32[4]{0:T(128)} %param.27) | copy-start | bytes 52
  7.4 2.8 %copy-start.11 = (f32[4,4,128]{2,1,0:T(4,128)S(1)}, f32[4,4,128]{2,1,0:T(4,128)}, u32[]{:S(2)}) copy-start(f32[4,4,128]{2,1,0:T(4,128)} %b_ref.6) | copy-start | bytes 24580
  7.4 2.8 %copy-start.10 = (f32[4,4,128]{2,1,0:T(4,128)S(1)}, f32[4,4,128]{2,1,0:T(4,128)}, u32[]{:S(2)}) copy-start(f32[4,4,128]{2,1,0:T(4,128)} %g_ref.6) | copy-start | bytes 24580
  7.4 17.2 %collective-permute-start = (f32[1,4,128,128]{3,2,1,0:T(8,128)S(1)}, f32[1,4,128,128]{3,2,1,0:T(8,128)S(1)}, u32[]{:S(2)}, u32[]{:S(2)}) collective-permute-start(f32[1,4,128,128]{3,2,1,0:T(8,128)S(1)} %get-tuple-element.31), channel_id=1, source_target_pairs={{0,4},{4,8},{8,12},{12,0},{1,5},{5,9},{9,13},{13,1},{2,6},{6,10},{... | collective-permute-start | bytes 786440 | tf_op jit(solution)/shard_map/ppermute | solution.py:321
  7.7 37.0 %collective-permute-start.1 = (f32[1,4,128,128]{3,2,1,0:T(8,128)S(1)}, f32[1,4,128,128]{3,2,1,0:T(8,128)S(1)}, u32[]{:S(2)}, u32[]{:S(2)}) collective-permute-start(f32[1,4,128,128]{3,2,1,0:T(8,128)S(1)} %get-tuple-element.31), channel_id=1, source_target_pairs={{0,8},{4,12},{8,0},{12,4},{1,9},{5,13},{9,1},{13,5},{2,10},{6,14},... | collective-permute-start | bytes 786440 | tf_op jit(solution)/shard_map/ppermute | solution.py:321
  9.4 35.3 %collective-permute-start.2 = (f32[1,4,128,128]{3,2,1,0:T(8,128)S(1)}, f32[1,4,128,128]{3,2,1,0:T(8,128)S(1)}, u32[]{:S(2)}, u32[]{:S(2)}) collective-permute-start(f32[1,4,128,128]{3,2,1,0:T(8,128)S(1)} %get-tuple-element.31), channel_id=1, source_target_pairs={{0,12},{4,0},{8,4},{12,8},{1,13},{5,1},{9,5},{13,9},{2,14},{6,2},{... | collective-permute-start | bytes 786440 | tf_op jit(solution)/shard_map/ppermute | solution.py:321
  21.2 34.9 %collective-permute-start.3 = (f32[1,4,128,128]{3,2,1,0:T(8,128)S(1)}, f32[1,4,128,128]{3,2,1,0:T(8,128)S(1)}, u32[]{:S(2)}, u32[]{:S(2)}) collective-permute-start(f32[1,4,128,128]{3,2,1,0:T(8,128)S(1)} %get-tuple-element.47), channel_id=1, source_target_pairs={{0,4},{4,8},{8,12},{12,0},{1,5},{5,9},{9,13},{13,1},{2,6},{6,10},{... | collective-permute-start | bytes 786440 | tf_op jit(solution)/shard_map/ppermute | solution.py:321
  24.6 31.5 %collective-permute-start.4 = (f32[1,4,128,128]{3,2,1,0:T(8,128)S(1)}, f32[1,4,128,128]{3,2,1,0:T(8,128)S(1)}, u32[]{:S(2)}, u32[]{:S(2)}) collective-permute-start(f32[1,4,128,128]{3,2,1,0:T(8,128)S(1)} %get-tuple-element.49), channel_id=1, source_target_pairs={{0,8},{4,12},{8,0},{12,4},{1,9},{5,13},{9,1},{13,5},{2,10},{6,14},... | collective-permute-start | bytes 786440 | tf_op jit(solution)/shard_map/ppermute | solution.py:321
  24.6 20.1 %copy-start.2 = (bf16[4,128,512]{2,1,0:T(8,128)(2,1)S(1)}, bf16[4,128,512]{2,1,0:T(8,128)(2,1)}, u32[]{:S(2)}) copy-start(bf16[4,128,512]{2,1,0:T(8,128)(2,1)} %v_ref.4) | copy-start | bytes 1572868
  24.6 31.5 %collective-permute-start.5 = (f32[1,4,128,128]{3,2,1,0:T(8,128)S(1)}, f32[1,4,128,128]{3,2,1,0:T(8,128)S(1)}, u32[]{:S(2)}, u32[]{:S(2)}) collective-permute-start(f32[1,4,128,128]{3,2,1,0:T(8,128)S(1)} %get-tuple-element.48), channel_id=1, source_target_pairs={{0,12},{4,0},{8,4},{12,8},{1,13},{5,1},{9,5},{13,9},{2,14},{6,2},{... | collective-permute-start | bytes 786440 | tf_op jit(solution)/shard_map/ppermute | solution.py:321
  56.0 1.0 %copy-start.5 = (bf16[1,256,512]{2,1,0:T(8,128)(2,1)S(1)}, bf16[1,256,512]{2,1,0:T(8,128)(2,1)}, u32[]{:S(2)}) copy-start(bf16[1,256,512]{2,1,0:T(8,128)(2,1)} %k_ref.7) | copy-start | bytes 786436
  56.0 1.0 %copy-start.7 = (bf16[1,256,512]{2,1,0:T(8,128)(2,1)S(1)}, bf16[1,256,512]{2,1,0:T(8,128)(2,1)}, u32[]{:S(2)}) copy-start(bf16[1,256,512]{2,1,0:T(8,128)(2,1)} %v_ref.5) | copy-start | bytes 786436
  56.0 1.1 %copy-start.8 = (bf16[1,256,512]{2,1,0:T(8,128)(2,1)S(1)}, bf16[1,256,512]{2,1,0:T(8,128)(2,1)}, u32[]{:S(2)}) copy-start(bf16[1,256,512]{2,1,0:T(8,128)(2,1)} %q_ref.5) | copy-start | bytes 786436
  56.1 1.2 %copy-start.9 = (bf16[1,256,512]{2,1,0:T(8,128)(2,1)S(1)}, bf16[1,256,512]{2,1,0:T(8,128)(2,1)}, u32[]{:S(2)}) copy-start(bf16[1,256,512]{2,1,0:T(8,128)(2,1)} %d_ref.5) | copy-start | bytes 786436
  56.1 1.1 %copy-start.15 = (f32[1,4,256]{2,1,0:T(4,128)S(1)}, f32[1,4,256]{2,1,0:T(4,128)}, u32[]{:S(2)}) copy-start(f32[1,4,256]{2,1,0:T(4,128)} %b_ref.7) | copy-start | bytes 12292
  56.2 1.0 %copy-start.13 = (f32[1,4,256]{2,1,0:T(4,128)S(1)}, f32[1,4,256]{2,1,0:T(4,128)}, u32[]{:S(2)}) copy-start(f32[1,4,256]{2,1,0:T(4,128)} %g_ref.7) | copy-start | bytes 12292
